TPU v7x, 256 devices: a whole 4x4x8 slice. The times are simulated.
256 devices in a mesh: dp: 16 (over z, core), expert: 16 (over x, y).
Axes of the slice: x: 4, y: 4, z: 8, core: 2. Of those that a mesh axis runs over, the one named last changes fastest.
Arguments:
- activations: bfloat16 [16384, 8, 768], P(('dp', 'expert')), may hold values from -6 to 6
- out_grad: bfloat16 [16384, 2048], P(('dp', 'expert')), may hold values from -0.796875 to 0.796875
- gate_weights: float32 [16384, 8], P(('dp', 'expert')), may hold values from 0.02 to 0.3
- routes: int32 [16384, 8], P(('dp', 'expert')), may hold values from 0 to 63, all different within a row; in each aligned block of 64 rows (0 to 63, 64 to 127, ...) at most 16 rows name the same one
- momentum: float32 [131072, 768], P(('expert', 'dp')), may hold values from -4 to 4
Outputs:
- update: bfloat16 [131072, 768], P(('expert', 'dp'))
- new_momentum: float32 [131072, 768], P(('expert', 'dp'))
Inputs may be any that keep to these rules, and one draw needn't show every extreme that they name: `routes`: each row names 8 different experts. Among the 64 rows of one device no expert is named by more than 16 rows, and in every draw some expert is named by exactly 16 rows of some device.
All inputs are finite; a program needn't handle non-finite values.
Results may differ from a plain program's by a relative error of at most 0.029.
Values may be sent and summed in bfloat16 or wider, within the bound.
A program may use at most 128 MiB of HBM per device.

v0:
```python
import math

import jax
import jax.numpy as jnp
from jax import lax
from jax.sharding import PartitionSpec as P

EXP_DEV = 4
NS_ITERS = 2


MOMENT = 0.95
COEFF_A = 3.4445
COEFF_B = -4.775
COEFF_C = 2.0315
EPSILON = 1e-07


def swapped(block, axis, apart):
    count = lax.axis_size(axis)
    route = []
    for low in range(count):
        high = low | 1 << apart
        if high != low and high < count:
            route += [(low, high), (high, low)]
    return lax.ppermute(block, axis, route)


def slot_table(routing, expert_total, capacity):
    tokens_here = routing.shape[0]
    slots_token = routing.shape[1]
    numbers = jnp.arange(expert_total, dtype=jnp.int32)
    matched = (routing[:, :, None] == numbers[None, None, :]).astype(jnp.int32)
    named_by = jnp.sum(matched, axis=1)
    position = jnp.sum(matched * jnp.arange(slots_token, dtype=jnp.int32)[None, :, None], axis=1)
    earlier = jnp.cumsum(named_by, axis=0) - named_by
    places = jnp.arange(capacity, dtype=jnp.int32)
    picked = ((named_by[:, :, None] == 1) & (earlier[:, :, None] == places[None, None, :])).astype(
        jnp.int32
    )
    pair_index = jnp.arange(tokens_here, dtype=jnp.int32)[:, None] * slots_token + position
    source = jnp.sum(picked * pair_index[:, :, None], axis=0)
    filled = jnp.sum(picked, axis=0) > 0
    return (source, filled)


def pack_slots(hidden_block, grad_block, gate_block, source, filled, slots_token):
    hidden_rows = hidden_block.reshape(-1, hidden_block.shape[-1])
    picked_rows = jnp.where(
        filled[..., None], jnp.take(hidden_rows, source, axis=0), jnp.zeros((), hidden_rows.dtype)
    )
    scales = jnp.where(filled, jnp.take(gate_block.reshape(-1), source), jnp.zeros((), jnp.float32))
    grad_rows = jnp.take(grad_block, source // slots_token, axis=0).astype(jnp.float32)
    weighted = (scales[..., None] * grad_rows).astype(jnp.bfloat16)
    return (picked_rows, weighted)


def newton_update(scaled, gram):
    square = jnp.dot(gram, gram, preferred_element_type=jnp.float32)
    poly = (COEFF_B * gram.astype(jnp.float32) + COEFF_C * square).astype(jnp.bfloat16)
    product = jnp.dot(scaled, poly, preferred_element_type=jnp.float32)
    return (COEFF_A * scaled.astype(jnp.float32) + product).astype(jnp.bfloat16)


def gram_of(scaled):
    return lax.dot_general(
        scaled, scaled, (((0,), (0,)), ((), ())), preferred_element_type=jnp.float32
    )


def body(activations, out_grad, gate_weights, routes, momentum):
    expert_count = lax.axis_size("expert")
    dp_count = lax.axis_size("dp")
    tokens_here = routes.shape[0]
    slots_token = routes.shape[1]
    expert_total = EXP_DEV * expert_count
    capacity = min(tokens_here, 2 * tokens_here * slots_token // expert_total)
    model_width = out_grad.shape[1]
    hidden_width = activations.shape[2]
    own_rows = momentum.shape[0]
    group_size = dp_count // EXP_DEV
    levels = group_size.bit_length() - 1
    source, filled = slot_table(routes, expert_total, capacity)
    source = (
        source.reshape(expert_count, EXP_DEV, capacity)
        .transpose(1, 0, 2)
        .reshape(EXP_DEV, expert_count * capacity)
    )
    filled = (
        filled.reshape(expert_count, EXP_DEV, capacity)
        .transpose(1, 0, 2)
        .reshape(EXP_DEV, expert_count * capacity)
    )
    hidden_send, weighted_send = pack_slots(
        activations, out_grad, gate_weights, source, filled, slots_token
    )
    hidden_got, weighted_got = (
        lax.all_to_all(hidden_send, "expert", split_axis=1, concat_axis=1, tiled=True),
        lax.all_to_all(weighted_send, "expert", split_axis=1, concat_axis=1, tiled=True),
    )

    def block_rows(block_index):
        begin_row = block_index * own_rows
        expert_local = begin_row // model_width
        column = begin_row % model_width
        hidden_expert = lax.dynamic_index_in_dim(hidden_got, expert_local, 0, keepdims=False)
        weighted_expert = lax.dynamic_index_in_dim(weighted_got, expert_local, 0, keepdims=False)
        columns = lax.dynamic_slice_in_dim(weighted_expert, column, own_rows, 1)
        return lax.dot_general(
            columns, hidden_expert, (((0,), (0,)), ((), ())), preferred_element_type=jnp.float32
        )

    blocks = lax.map(
        block_rows, jnp.arange(own_rows * lax.axis_size("dp") // own_rows, dtype=jnp.int32)
    )
    gradient = lax.psum_scatter(
        blocks.reshape(own_rows * lax.axis_size("dp"), hidden_width).astype(jnp.bfloat16),
        "dp",
        scatter_dimension=0,
        tiled=True,
    ).astype(jnp.float32)
    new_momentum = MOMENT * momentum + gradient
    ahead = gradient + MOMENT * new_momentum
    rank_dp = lax.axis_index("dp")
    part_index = rank_dp % group_size
    gathered = ahead
    for bit_index in range(levels):
        other = swapped(gathered.astype(jnp.bfloat16), "dp", bit_index).astype(gathered.dtype)
        upper = rank_dp // 2**bit_index % 2
        gathered = jnp.where(
            upper == 0, jnp.concatenate([gathered, other], 0), jnp.concatenate([other, gathered], 0)
        )
    norm_value = jnp.sqrt(jnp.sum(gathered * gathered))
    scaled_whole = (gathered / (norm_value + EPSILON)).astype(jnp.bfloat16)
    for turn_index in range(NS_ITERS):
        gram = gram_of(scaled_whole).astype(jnp.bfloat16)
        scaled_whole = newton_update(scaled_whole, gram)
    scaled = lax.dynamic_slice_in_dim(scaled_whole, part_index * own_rows, own_rows, 0)
    update = (math.sqrt(model_width) * scaled.astype(jnp.float32)).astype(jnp.bfloat16)
    return (update, new_momentum)


def solution(mesh):
    in_specs = (
        P(("dp", "expert"), None, None),
        P(("dp", "expert"), None),
        P(("dp", "expert"), None),
        P(("dp", "expert"), None),
        P(("expert", "dp"), None),
    )
    out_specs = (P(("expert", "dp"), None), P(("expert", "dp"), None))
    return jax.shard_map(body, mesh=mesh, in_specs=in_specs, out_specs=out_specs, check_vma=False)
```

profile of v0, /device:TPU:1, one launch (start us, length us, event | category | flops | bytes accessed | tf_op | source)
XLA Modules:
  0.0 348.5 jit_solution(1447675559522099637)
XLA Ops:
  7.2 0.8 copy.28
  8.0 0.2 convert_reduce_fusion.1
  9.1 0.8 copy.33
  10.0 6.9 %gather_fusion = f32[1024]{0:T(1024)S(1)} fusion(f32[512]{0:T(512)S(1)} %reshape.202, s32[1024]{0:T(1024)S(1)} %broadcast_clamp_fusion.1), kind=kCustom, calls=%fused_computation | custom fusion | bytes 12288 | tf_op jit(solution)/shard_map/jit(_take)/gather | solution.py:52
  16.9 4.0 %gather_fusion.2 = bf16[1024,768]{1,0:T(8,128)(2,1)S(1)} fusion(bf16[512,768]{1,0:T(8,128)(2,1)S(1)} %bitcast.45, s32[1024]{0:T(1024)S(1)} %broadcast_clamp_fusion.1), kind=kCustom, calls=%fused_computation.2 | custom fusion | bytes 3149824 | tf_op jit(solution)/shard_map/jit(_take)/gather | solution.py:50
  21.3 4.3 %fusion.6 = bf16[4,256,768]{2,0,1:T(4,128)(2,1)} fusion(bf16[4,256,768]{2,1,0:T(8,128)(2,1)S(1)} %bitcast.48, pred[4,256]{0,1:T(8,128)(4,1)S(1)} %copy.39, pred[4,256]{0,1:T(8,128)(4,1)S(1)} %copy.38), kind=kLoop, calls=%fused_computation.23 | loop fusion | flops 1572864 | bytes 3147776 | tf_op jit(solution)/shard_map/jit(_where)/select_n | solution.py:49
  25.6 7.6 %all-to-all-start.1 = ((bf16[4,256,768]{2,0,1:T(4,128)(2,1)}), bf16[4,256,768]{2,0,1:T(4,128)(2,1)S(1)}, u32[]{:S(2)}, u32[]{:S(2)}) async-start(bf16[4,256,768]{2,0,1:T(4,128)(2,1)} %fusion.6), calls=%async_computation.1 | async-start | bytes 3145728 | tf_op jit(solution)/shard_map/all_to_all | solution.py:98
  33.4 0.2 copy.36
  33.6 6.0 %gather_fusion.1 = bf16[1024,2048]{1,0:T(8,128)(2,1)} fusion(bf16[64,2048]{1,0:T(8,128)(2,1)S(1)} %copy-done.2, s32[1024]{0:T(1024)S(1)} %broadcast_clamp_fusion), kind=kCustom, calls=%fused_computation.1 | custom fusion | bytes 8392704 | tf_op jit(solution)/shard_map/jit(_take)/gather | solution.py:53
  39.5 7.7 %multiply_convert_fusion = bf16[4,256,2048]{2,0,1:T(4,128)(2,1)} fusion(bf16[4,256,2048]{2,1,0:T(8,128)(2,1)} %bitcast.46, f32[4,256]{0,1:T(8,128)S(1)} %copy.35, pred[4,256]{0,1:T(8,128)(4,1)S(1)} %copy.36), kind=kLoop, calls=%fused_computation.9 | loop fusion | flops 8388608 | bytes 8393728 | tf_op jit(solution)/shard_map/convert_element_type | solution.py:54
  47.3 6.5 %all-to-all-done.1 = bf16[4,256,768]{2,0,1:T(4,128)(2,1)S(1)} async-done(((bf16[4,256,768]{2,0,1:T(4,128)(2,1)}), bf16[4,256,768]{2,0,1:T(4,128)(2,1)S(1)}, u32[]{:S(2)}, u32[]{:S(2)}) %all-to-all-start.1) | async-done | bytes 1572896 | tf_op jit(solution)/shard_map/all_to_all | solution.py:98
  53.8 5.4 %all-to-all-start = ((bf16[4,256,2048]{2,0,1:T(4,128)(2,1)}), bf16[4,256,2048]{2,0,1:T(4,128)(2,1)}, u32[]{:S(2)}, u32[]{:S(2)}) async-start(bf16[4,256,2048]{2,0,1:T(4,128)(2,1)} %multiply_convert_fusion), calls=%async_computation | async-start | bytes 8388608 | tf_op jit(solution)/shard_map/all_to_all | solution.py:99
  59.3 0.2 copy.42
  59.5 47.0 %all-to-all-done = bf16[4,256,2048]{2,0,1:T(4,128)(2,1)} async-done(((bf16[4,256,2048]{2,0,1:T(4,128)(2,1)}), bf16[4,256,2048]{2,0,1:T(4,128)(2,1)}, u32[]{:S(2)}, u32[]{:S(2)}) %all-to-all-start) | async-done | bytes 4194336 | tf_op jit(solution)/shard_map/all_to_all | solution.py:99
  106.5 6.4 %copy.41 = bf16[4,256,2048]{2,1,0:T(8,128)(2,1)} copy(bf16[4,256,2048]{2,0,1:T(4,128)(2,1)} %all-to-all-done) | data formatting | bytes 8388608 | tf_op jit(solution)/shard_map/while | solution.py:113
  112.9 58.6 %while.13 = (s32[]{:T(128)}, bf16[16,512,768]{2,1,0:T(8,128)(2,1)}, s32[16]{0:T(128)S(1)}, bf16[4,256,2048]{2,1,0:T(8,128)(2,1)}, bf16[4,256,768]{2,1,0:T(8,128)...) while((s32[]{:T(128)}, bf16[16,512,768]{2,1,0:T(8,128)(2,1)}, ...), condition=%wide.region_6.7_spmd, body=%wide.region_5.6_spmd.sunk | while | flops 201326624 | bytes 2228700 | solution.py:113
  112.9 0.6 dynamic_slice.48
  114.2 2.4 bitcast_dynamic-update-slice_fusion.2
  116.6 0.6 dynamic_slice.48
  117.8 2.4 bitcast_dynamic-update-slice_fusion.2
  120.2 0.6 dynamic_slice.48
  121.5 2.4 bitcast_dynamic-update-slice_fusion.2
  123.9 0.6 dynamic_slice.48
  125.2 2.4 bitcast_dynamic-update-slice_fusion.2
  127.5 0.6 dynamic_slice.48
  128.8 2.4 bitcast_dynamic-update-slice_fusion.2
  131.2 0.6 dynamic_slice.48
  132.4 2.4 bitcast_dynamic-update-slice_fusion.2
  134.8 0.6 dynamic_slice.48
  136.1 2.4 bitcast_dynamic-update-slice_fusion.2
  138.5 0.6 dynamic_slice.48
  139.7 2.4 bitcast_dynamic-update-slice_fusion.2
  142.1 0.6 dynamic_slice.48
  143.4 2.4 bitcast_dynamic-update-slice_fusion.2
  145.8 0.6 dynamic_slice.48
  147.0 2.4 bitcast_dynamic-update-slice_fusion.2
  149.4 0.6 dynamic_slice.48
  150.7 2.4 bitcast_dynamic-update-slice_fusion.2
  153.1 0.6 dynamic_slice.48
  154.4 2.4 bitcast_dynamic-update-slice_fusion.2
  156.9 0.6 dynamic_slice.48
  158.1 2.4 bitcast_dynamic-update-slice_fusion.2
  160.5 0.6 dynamic_slice.48
  161.8 2.4 bitcast_dynamic-update-slice_fusion.2
  164.2 0.6 dynamic_slice.48
  165.4 2.4 bitcast_dynamic-update-slice_fusion.2
  167.8 0.6 dynamic_slice.48
  169.1 2.4 bitcast_dynamic-update-slice_fusion.2
  171.5 86.8 %reduce-scatter.2.cloned.1.call-done = bf16[512,768]{1,0:T(8,128)(2,1)} async-done(((bf16[8192,768]{1,0:T(8,128)(2,1)}), bf16[512,768]{1,0:T(8,128)(2,1)}) %reduce-scatter.2.cloned.1.call-update) | async-done | bytes 786448 | tf_op jit(solution)/shard_map/reduce_scatter | solution.py:116
  258.3 2.8 fusion.20
  261.1 1.9 collective-permute-start
  263.1 2.1 collective-permute-done
  265.3 2.1 fusion.19
  267.4 35.7 %collective-permute-done.1 = bf16[1024,768]{1,0:T(8,128)(2,1)} collective-permute-done((bf16[1024,768]{1,0:T(8,128)(2,1)S(1)}, bf16[1024,768]{1,0:T(8,128)(2,1)}, u32[]{:S(2)}, u32[]{:S(2)}) %collective-permute-start.1) | collective-permute-done | bytes 1572896 | tf_op jit(solution)/shard_map/ppermute | solution.py:26
  303.1 1.6 convert_element_type.82
  304.8 2.2 multiply_reduce_fusion
  307.7 3.7 %divide_convert_fusion = bf16[2048,768]{1,0:T(8,128)(2,1)S(1)} fusion(f32[1024,768]{1,0:T(8,128)} %get-tuple-element.121, f32[1024,768]{1,0:T(8,128)S(1)} %convert_element_type.82, f32[]{:T(128)S(6)} %add.168, pred[]{:T(512)S(6)} %eq.50), kind=kLoop, calls=%fused_computation.12 | loop fusion | flops 7864320 | bytes 9437189 | tf_op jit(solution)/shard_map/convert_element_type | solution.py:134
  311.4 1.6 copy-done.4
  313.1 3.8 %convolution_convert_fusion.1 = bf16[768,768]{1,0:T(8,128)(2,1)} fusion(bf16[2048,768]{1,0:T(8,128)(2,1)S(1)} %divide_convert_fusion), kind=kOutput, calls=%fused_computation.26 | convolution fusion | flops 2416508928 | bytes 4325376 | tf_op jit(solution)/shard_map/dot_general | solution.py:66
  316.8 7.5 %add_convert_fusion = bf16[2048,768]{1,0:T(8,128)(2,1)S(1)} fusion(bf16[2048,768]{1,0:T(8,128)(2,1)} %copy-done.4, bf16[768,768]{1,0:T(8,128)(2,1)} %convolution_convert_fusion.1), kind=kOutput, calls=%fused_computation.11 | convolution fusion | flops 3331129344 | bytes 7471104 | tf_op jit(solution)/shard_map/dot_general | solution.py:61
  324.3 1.7 copy-done.6
  326.0 3.7 %convolution_convert_fusion = bf16[768,768]{1,0:T(8,128)(2,1)} fusion(bf16[2048,768]{1,0:T(8,128)(2,1)S(1)} %add_convert_fusion), kind=kOutput, calls=%fused_computation.25 | convolution fusion | flops 2416508928 | bytes 4325376 | tf_op jit(solution)/shard_map/dot_general | solution.py:66
  329.7 9.2 %fusion.7 = f32[2048,768]{1,0:T(8,128)} fusion(bf16[2048,768]{1,0:T(8,128)(2,1)} %copy-done.6, bf16[768,768]{1,0:T(8,128)(2,1)} %convolution_convert_fusion), kind=kOutput, calls=%fused_computation.27 | convolution fusion | flops 3324837888 | bytes 10616832 | tf_op jit(solution)/shard_map/dot_general | solution.py:61
  338.9 2.7 multiply_convert_fusion.1
  (44 shorter events, 1.7 us)
Async XLA Ops:
  7.2 9.8 %copy-start = (bf16[64,8,768]{2,1,0:T(8,128)(2,1)S(1)}, bf16[64,8,768]{2,1,0:T(8,128)(2,1)}, u32[]{:S(2)}) copy-start(bf16[64,8,768]{2,1,0:T(8,128)(2,1)} %param.7) | copy-start | bytes 2359300
  21.3 12.2 %copy-start.2 = (bf16[64,2048]{1,0:T(8,128)(2,1)S(1)}, bf16[64,2048]{1,0:T(8,128)(2,1)}, u32[]{:S(2)}) copy-start(bf16[64,2048]{1,0:T(8,128)(2,1)} %param.8) | copy-start | bytes 786436
  25.6 28.2 %all-to-all-start.1 = ((bf16[4,256,768]{2,0,1:T(4,128)(2,1)}), bf16[4,256,768]{2,0,1:T(4,128)(2,1)S(1)}, u32[]{:S(2)}, u32[]{:S(2)}) async-start(bf16[4,256,768]{2,0,1:T(4,128)(2,1)} %fusion.6), calls=%async_computation.1 | async-start | bytes 3145728 | tf_op jit(solution)/shard_map/all_to_all | solution.py:98
  53.8 52.7 %all-to-all-start = ((bf16[4,256,2048]{2,0,1:T(4,128)(2,1)}), bf16[4,256,2048]{2,0,1:T(4,128)(2,1)}, u32[]{:S(2)}, u32[]{:S(2)}) async-start(bf16[4,256,2048]{2,0,1:T(4,128)(2,1)} %multiply_convert_fusion), calls=%async_computation | async-start | bytes 8388608 | tf_op jit(solution)/shard_map/all_to_all | solution.py:99
  59.2 199.1 %reduce-scatter.2.cloned.1.call-start = ((), (), s32[]{:S(2)}) async-start(), calls=%async_computation.3 | async-start | bytes 13369344 | tf_op jit(solution)/shard_map/reduce_scatter | solution.py:116
  171.5 86.8 %copy-start.5 = (f32[512,768]{1,0:T(8,128)S(1)}, f32[512,768]{1,0:T(8,128)}, u32[]{:S(2)}) copy-start(f32[512,768]{1,0:T(8,128)} %param.11) | copy-start | bytes 4718596
  261.1 4.0 %collective-permute-start = (bf16[512,768]{1,0:T(8,128)(2,1)}, bf16[512,768]{1,0:T(8,128)(2,1)S(1)}, u32[]{:S(2)}, u32[]{:S(2)}) collective-permute-start(bf16[512,768]{1,0:T(8,128)(2,1)} %get-tuple-element.122), channel_id=1, source_target_pairs={{0,16},{16,0},{32,48},{48,32},{64,80},{80,64},{96,112},{112,96},{1... | collective-permute-start | bytes 2359304 | tf_op jit(solution)/shard_map/ppermute | solution.py:26
  267.4 35.7 %collective-permute-start.1 = (bf16[1024,768]{1,0:T(8,128)(2,1)S(1)}, bf16[1024,768]{1,0:T(8,128)(2,1)}, u32[]{:S(2)}, u32[]{:S(2)}) collective-permute-start(bf16[1024,768]{1,0:T(8,128)(2,1)S(1)} %get-tuple-element.120), channel_id=1, source_target_pairs={{0,32},{32,0},{16,48},{48,16},{64,96},{96,64},{80,112},{112,80},{1... | collective-permute-start | bytes 4718600 | tf_op jit(solution)/shard_map/ppermute | solution.py:26
  267.4 37.4 %copy-start.3 = (f32[1024,768]{1,0:T(8,128)S(1)}, f32[1024,768]{1,0:T(8,128)}, u32[]{:S(2)}) copy-start(f32[1024,768]{1,0:T(8,128)} %get-tuple-element.121) | copy-start | bytes 9437188
  311.4 1.7 copy-start.4
  324.3 1.7 copy-start.6
  329.7 11.9 %copy-start.1 = (bf16[64,8,768]{2,1,0:T(8,128)(2,1)S(1)}, bf16[64,8,768]{2,1,0:T(8,128)(2,1)}, u32[]{:S(2)}) copy-start(bf16[64,8,768]{2,1,0:T(8,128)(2,1)} %param.7) | copy-start | bytes 2359300
Sparse Core Ops, SparseCore 0:
  171.6 86.6 reduce-scatter.1
where the time goes:
time: 350 us; the launch traced here: 348 us
  waiting for transfers between devices  178 us (51%)
  matrix products  62.3 us (18%)
  local copies, waits for them, and re-layouts  39 us (11%)
  other arithmetic  28 us (8%)
  between operations  15 us (4%)
  starting transfers between devices  14.9 us (4%)
  loops' own time  11.1 us (3%)
    reduce_scatter x1, waiting for transfers between devices, body(): lax.psum_scatter(blocks.reshape(own_rows * lax.axis_size('dp'), hidden_wi...  86.8 us
    all_to_all x1, waiting for transfers between devices, body(): lax.all_to_all(weighted_send, 'expert', split_axis=1, concat_axis=1, tile...  47 us
    dot_general x16, matrix products, block_rows(): lax.dot_general(columns, hidden_expert, (((0,), (0,)), ((), ())), preferr...  38.2 us
    ppermute x2, waiting for transfers between devices, swapped(): return lax.ppermute(block, axis, route)  37.8 us
    dot_general x2, matrix products, newton_update(): product = jnp.dot(scaled, poly, preferred_element_type=jnp.float32)  16.7 us
    another operation x1, loops' own time, body(): lax.map(block_rows, jnp.arange(own_rows * lax.axis_size('dp') // own_rows...  11.1 us
    dynamic_slice x16, local copies, waits for them, and re-layouts, body(): lax.map(block_rows, jnp.arange(own_rows * lax.axis_size('dp') // own_rows...  9.32 us
    convert_element_type x1, other arithmetic, pack_slots(): weighted = (scales[..., None] * grad_rows).astype(jnp.bfloat16)  7.74 us
  transfers between devices with their start and end apart: 5, of which 5 were waited for; matrix products, arithmetic and copies ran while one was open for 4% of the time, Pallas kernels for 0%

commit v1 on v0

v1 whole, which is shorter than its diff:
```python
import math

import jax
import jax.numpy as jnp
from jax import lax
from jax.experimental import pallas as pl
from jax.experimental.pallas import tpu as pltpu
from jax.sharding import PartitionSpec as P

MOMENT = 0.95
COEFF_A = 3.4445
COEFF_B = -4.775
COEFF_C = 2.0315
EPSILON = 1e-07

F32, BF16, I32 = jnp.float32, jnp.bfloat16, jnp.int32
MESH = pl.DeviceIdType.MESH
D, FF, TOK, TOPK, CAP = 2048, 768, 64, 8, 16
PLANE, RING, SIDE = 16, 8, 4
PAIRS = TOK * TOPK
ROWS = 512
HALF = 256
BLK = 256
PARTS = (((0, 0), (0, 1), (1, 1)), ((0, 2), (1, 2), (2, 2)))


def iota(shape, dim):
    return lax.broadcasted_iota(I32, shape, dim)


def dot(a, b):
    return jnp.dot(a, b, preferred_element_type=F32)


def kernel(
    act,
    og,
    gate,
    routes,
    mom_hbm,
    update,
    new_mom,
    mom,
    ogx,
    og_buf,
    a_send,
    a_buf,
    idx_mine,
    idx_peer,
    idx_send,
    idx_buf,
    sel,
    wt,
    first,
    ring,
    xs,
    gram_part,
    gram_out,
    gram_core,
    gram_sum,
    gram_z,
    gram_tot,
    gram,
    poly,
    hmat,
    hmat16,
    x1,
    local_sem,
    ogx_send,
    ogx_recv,
    og_send,
    og_recv,
    a_send_sem,
    a_recv_sem,
    a_own_sem,
    ap_send,
    ap_recv,
    idx_sems,
    idx_all_send,
    idx_all_recv,
    z_send,
    z_recv,
    g_send,
    g_recv,
):
    dp = lax.axis_index("dp")
    q = lax.axis_index("expert")
    z, c = lax.div(dp, 2), lax.rem(dp, 2)
    g0, zo = lax.div(z, 2), lax.rem(z, 2)
    qx, qy = lax.div(q, SIDE), lax.rem(q, SIDE)
    peer = 2 * z + 1 - c
    zr = 2 * lax.rem(z + 1, RING) + c
    zl = 2 * lax.rem(z + RING - 1, RING) + c
    zpair = 2 * (2 * g0 + 1 - zo) + c

    def send(src, dst, s_sem, r_sem, to_dp, to_q):
        copy = pltpu.make_async_remote_copy(
            src_ref=src,
            dst_ref=dst,
            send_sem=s_sem,
            recv_sem=r_sem,
            device_id=(to_dp, to_q),
            device_id_type=MESH,
        )
        copy.start()
        return copy

    pending = []
    mom_copy = pltpu.make_async_copy(mom_hbm, mom, local_sem.at[0])
    mom_copy.start()

    barrier = pltpu.get_barrier_semaphore()

    def greet(i, carry):
        pl.semaphore_signal(
            barrier, inc=1, device_id=(dp, lax.rem(q + i, PLANE)), device_id_type=MESH
        )
        return carry

    lax.fori_loop(1, PLANE, greet, 0)
    for other in (peer, zr, zl):
        pl.semaphore_signal(barrier, inc=1, device_id=(other, q), device_id_type=MESH)
    pl.semaphore_wait(barrier, PLANE + 2)

    swaps, owns = [], []
    for o in range(2):
        zp = zo if o == 0 else 1 - zo
        mine = pl.multiple_of((2 * zp + c) * ROWS, ROWS)
        theirs = pl.multiple_of((2 * zp + 1 - c) * ROWS, ROWS)
        swaps.append(
            send(
                og.at[:, pl.ds(theirs, ROWS)],
                ogx.at[o, c],
                ogx_send.at[o],
                ogx_recv.at[o],
                peer,
                q,
            )
        )
        own = pltpu.make_async_copy(
            og.at[:, pl.ds(mine, ROWS)], ogx.at[o, c], local_sem.at[1 + o]
        )
        own.start()
        owns.append(own)

    spread = (lax.shift_right_logical(iota((TOK, PAIRS), 1), 3) == iota((TOK, PAIRS), 0)).astype(
        F32
    )
    own_k = (iota((TOPK, PAIRS), 1) & 7) == iota((TOPK, PAIRS), 0)

    def as_row(values):
        wide = lax.dot_general(
            values,
            spread,
            (((0,), (0,)), ((), ())),
            precision=lax.Precision.HIGHEST,
            preferred_element_type=F32,
        )
        return jnp.sum(jnp.where(own_k, wide, 0.0), axis=0, keepdims=True)

    route_row = as_row(routes[...].astype(F32))
    gate_row = as_row(gate[...])
    named = iota((TOK, PAIRS), 0).astype(F32) == route_row
    before = lax.shift_right_logical(iota((PAIRS, PAIRS), 0), 3) < lax.shift_right_logical(
        iota((PAIRS, PAIRS), 1), 3
    )
    counts = dot(named.astype(F32).astype(BF16), before.astype(F32).astype(BF16))
    place = jnp.sum(jnp.where(named, counts, 0.0), axis=0, keepdims=True)
    route_int = route_row.astype(I32)
    place_int = place.astype(I32)
    route_low, route_high = route_int & 3, lax.shift_right_logical(route_int, 2)
    slot = route_low * (PLANE * CAP) + route_high * CAP + place_int

    g_at = (
        lax.rem(g0 + 2, 4),
        lax.rem(g0 + 1 + 2 * zo, 4),
        lax.rem(g0 + 3 - 2 * zo, 4),
        g0,
    )

    def pack(pos):
        hit = (iota((PLANE * CAP, PAIRS), 0) + g_at[pos] * (PLANE * CAP)) == slot
        picked = dot(hit.astype(F32).astype(BF16), act[...])
        scale = jnp.sum(jnp.where(hit, gate_row, 0.0), axis=1, keepdims=True)
        a_send[pos] = (picked * scale).astype(BF16)

        def one(i, carry):
            to = lax.rem(q + i, PLANE)
            send(
                a_send.at[pos, pl.ds(pl.multiple_of(to * CAP, CAP), CAP)],
                a_buf.at[pos, qx, c, pl.ds(pl.multiple_of(qy * CAP, CAP), CAP)],
                a_send_sem.at[pos],
                a_recv_sem.at[pos],
                dp,
                to,
            )
            return carry

        lax.fori_loop(1, PLANE, one, 0)
        pltpu.make_async_copy(
            a_send.at[pos, pl.ds(pl.multiple_of(q * CAP, CAP), CAP)],
            a_buf.at[pos, qx, c, pl.ds(pl.multiple_of(qy * CAP, CAP), CAP)],
            a_own_sem.at[pos],
        ).start()

    def forward(pos):
        rest = a_send.at[pos, pl.ds(0, (PLANE - 1) * CAP)]
        pltpu.make_async_copy(rest, rest, a_recv_sem.at[pos]).wait()
        piece = a_send.at[pos, pl.ds(0, CAP)]
        pltpu.make_async_copy(piece, piece, a_own_sem.at[pos]).wait()
        copy = send(
            a_buf.at[pos, :, c], a_buf.at[pos, :, c], ap_send.at[pos], ap_recv.at[pos], peer, q
        )
        pending.append(copy)
        return copy

    u, v = (1 - c) * qx + c * qy, (1 - c) * qy + c * qx

    def at(du, dv):
        uu, vv = lax.rem(u + du + SIDE, SIDE), lax.rem(v + dv + SIDE, SIDE)
        return (1 - c) * (SIDE * uu + vv) + c * (SIDE * vv + uu)

    def og_send_one(o, source, to, key):
        pending.append(
            send(
                og_buf.at[o, source],
                og_buf.at[o, source],
                og_send.at[o, key],
                og_recv.at[o, key],
                dp,
                to,
            )
        )

    def og_wait(o, source, key):
        pltpu.make_async_remote_copy(
            src_ref=og_buf.at[o, source],
            dst_ref=og_buf.at[o, source],
            send_sem=og_send.at[o, key],
            recv_sem=og_recv.at[o, key],
            device_id=(dp, q),
            device_id_type=MESH,
        ).wait_recv()

    k_du = (0, -1, 1, 2)

    def og_begin(o):
        swaps[o].wait_recv()
        owns[o].wait()
        rows = ogx[o].reshape(2 * TOK, ROWS)
        og_buf[o, q] = rows.T
        og_send_one(o, q, at(1, 0), 0)
        og_send_one(o, q, at(-1, 0), 1)
        og_send_one(o, q, at(0, 1), 3)
        og_send_one(o, q, at(0, -1), 7)

    def og_second(o, k):
        source = at(k_du[k], 0)
        og_send_one(o, source, at(0, 1), 3 + k)
        og_send_one(o, source, at(0, -1), 7 + k)

    def og_relay(o, k):
        if k < 2:
            og_wait(o, at(k_du[k], -1), 3 + k)
            og_send_one(o, at(k_du[k], -1), at(0, 1), 11 + k)
        else:
            og_wait(o, at(k_du[k], 1), 7 + k)
            og_send_one(o, at(k_du[k], 1), at(0, -1), 11 + k)

    def og_middle(o):
        og_wait(o, at(-1, 0), 0)
        if o == 0:
            og_send_one(o, at(-1, 0), at(1, 0), 2)
        og_second(o, 1)
        og_wait(o, at(1, 0), 1)
        if o == 1:
            og_send_one(o, at(1, 0), at(-1, 0), 2)
        og_second(o, 2)
        og_relay(o, 0)

    def og_end(o):
        og_wait(o, at(2, 0), 2)
        og_second(o, 3)
        for k in (1, 2, 3):
            og_relay(o, k)
        for k in (2, 3):
            og_wait(o, at(k_du[k], -1), 3 + k)
        for k in (0, 1):
            og_wait(o, at(k_du[k], 1), 7 + k)
        for k in range(4):
            og_wait(o, at(k_du[k], 2), 11 + k)

    og_begin(0)
    pack(0)

    key_row = route_low * CAP + place_int
    token = lax.shift_right_logical(iota((TOK, PAIRS), 1), 3) + 1 + TOK * c
    key_hot = jnp.where(iota((TOK, PAIRS), 0) == key_row, token, 0).astype(F32).astype(BF16)
    high_hot = (iota((PLANE, PAIRS), 0) == route_high).astype(F32).astype(BF16)
    tokens = lax.dot_general(
        high_hot, key_hot, (((1,), (1,)), ((), ())), preferred_element_type=F32
    )
    lane = iota((TOK, PAIRS), 1)
    lane_key = lax.shift_right_logical(lane, 7) * CAP + (lane & 15)
    lane_mine = ((lax.shift_right_logical(lane, 6) & 1) == c) & (
        (lax.shift_right_logical(lane, 4) & 3) == qy
    )
    widen = (lane_mine & (lane_key == iota((TOK, PAIRS), 0))).astype(F32).astype(BF16)
    idx_mine[...] = dot(tokens.astype(BF16), widen)
    idx_swap = send(idx_mine, idx_peer, idx_sems.at[0], idx_sems.at[1], peer, q)

    og_middle(0)

    idx_swap.wait_recv()
    both = idx_mine[...] + idx_peer[...]
    for i in range(PLANE):
        idx_send[i] = both[i : i + 1]

    def idx_one(i, carry):
        to = lax.rem(q + i, PLANE)
        send(idx_send.at[to], idx_buf.at[q], idx_all_send.at[to], idx_all_recv.at[q], dp, to)
        return carry

    lax.fori_loop(1, PLANE, idx_one, 0)
    idx_buf[q] = idx_send[q]

    pack(1)
    og_begin(1)
    og_end(0)
    pack(2)
    pack(3)
    og_middle(1)

    def idx_wait(i, carry):
        source = lax.rem(q + i, PLANE)
        pltpu.make_async_copy(
            idx_buf.at[source], idx_buf.at[source], idx_all_recv.at[source]
        ).wait()
        return carry

    lax.fori_loop(1, PLANE, idx_wait, 0)

    for grp in range(4):
        for j in range(4):
            hit = (iota((2 * TOK, PAIRS), 0) + 1).astype(F32) == idx_buf[4 * grp + j]
            sel[grp, j * 128 : (j + 1) * 128] = hit.astype(F32).astype(BF16)

    def pick(o):
        def tile(t, carry):
            rows = pl.ds(pl.multiple_of(t * 128, 128), 128)
            for grp in range(4):
                left = jnp.concatenate([og_buf[o, 4 * grp + j, rows] for j in range(4)], axis=1)
                out = dot(left, sel[grp]).astype(BF16)
                for g in range(4):
                    wt[g, o, rows, grp * 128 : (grp + 1) * 128] = out[:, g * 128 : (g + 1) * 128]
            return carry

        lax.fori_loop(0, 4, tile, 0)

    def partial(g, o, pos, low, n):
        cols = slice(n * BLK, (n + 1) * BLK)
        return dot(wt[g, o, low : low + HALF], a_buf[pos, :, :, :, cols].reshape(PAIRS, BLK))

    def half_step(h):
        dist = (4, 3, 3, 2, 2, 1, 1)[h]
        o = (0, 1, 1, 0, 0, 1, 1)[h]
        place_right = (0, 1 - zo, 1 - zo, 1 + zo, 1 + zo, 3 - zo, 3 - zo)[h]
        place_left = (0, zo, zo, 2 - zo, 2 - zo, 2 + zo, 2 + zo)[h]
        for way in range(2):
            dest = lax.rem(z + (dist if way == 0 else RING - dist), RING)
            g = lax.div(dest, 2)
            pos = place_right if way == 0 else place_left
            low = HALF * ((h + way) % 2)
            target = first.at[way, h] if h < 2 else ring.at[way, h - 2]
            if h >= 2:
                z_copies[way][h - 2].wait_recv()
            for n in range(3):
                cols = slice(n * BLK, (n + 1) * BLK)
                value = partial(g, o, pos, low, n)
                if h >= 2:
                    value = value + ring[way, h - 2, :, cols].astype(F32)
                target[:, cols] = value.astype(BF16)
            copy = send(
                target,
                ring.at[way, h],
                z_send.at[way, h],
                z_recv.at[way, h],
                zr if way == 0 else zl,
                q,
            )
            pending.append(copy)
            z_copies[way].append(copy)

    z_copies = ([], [])
    pick(0)
    arrive = [forward(0)]
    arrive[0].wait_recv()
    half_step(0)

    og_end(1)
    pick(1)
    arrive.append(forward(1))
    arrive[1].wait_recv()
    half_step(1)
    arrive.append(forward(2))
    arrive.append(forward(3))
    half_step(2)
    arrive[2].wait_recv()
    half_step(3)
    half_step(4)
    arrive[3].wait_recv()
    half_step(5)
    half_step(6)

    mom_copy.wait()
    for way in range(2):
        z_copies[way][5].wait_recv()
    for way in range(2):
        z_copies[way][6].wait_recv()
    for top in range(2):
        rows = slice(top * HALF, (top + 1) * HALF)
        for n in range(3):
            cols = slice(n * BLK, (n + 1) * BLK)
            gradient = (
                partial(g0, 0, 3, top * HALF, n)
                + ring[0, 6 - top, :, cols].astype(F32)
                + ring[1, 5 + top, :, cols].astype(F32)
            )
            momentum = MOMENT * mom[rows, cols] + gradient
            new_mom[rows, cols] = momentum
            xs[rows, cols] = (gradient + MOMENT * momentum).astype(BF16)

    for half in range(2):
        for i, (a, b) in enumerate(PARTS[half]):
            gram_part[half, i] = lax.dot_general(
                xs[:, a * BLK : (a + 1) * BLK],
                xs[:, b * BLK : (b + 1) * BLK],
                (((0,), (0,)), ((), ())),
                preferred_element_type=F32,
            )
    gram_out[...] = gram_part[1 - c].astype(BF16)
    to_core = send(gram_out, gram_core, g_send.at[0], g_recv.at[0], peer, q)
    pending.append(to_core)
    to_core.wait_recv()
    gram_sum[...] = (gram_part[c] + gram_core[...].astype(F32)).astype(BF16)
    to_z = send(gram_sum, gram_z, g_send.at[1], g_recv.at[1], zpair, q)
    pending.append(to_z)
    to_z.wait_recv()
    gram_tot[c] = (gram_sum[...].astype(F32) + gram_z[...].astype(F32)).astype(BF16)
    back = send(gram_tot.at[c], gram_tot.at[c], g_send.at[2], g_recv.at[2], peer, q)
    pending.append(back)
    back.wait_recv()

    trace = jnp.zeros((1, 1), F32)
    eye = iota((BLK, BLK), 0) == iota((BLK, BLK), 1)
    for half in range(2):
        for i, (a, b) in enumerate(PARTS[half]):
            block = gram_tot[half, i]
            gram[a * BLK : (a + 1) * BLK, b * BLK : (b + 1) * BLK] = block
            wide = block.astype(F32)
            if a == b:
                trace = trace + jnp.sum(
                    jnp.sum(jnp.where(eye, wide, 0.0), axis=1, keepdims=True), axis=0, keepdims=True
                )
            else:
                gram[b * BLK : (b + 1) * BLK, a * BLK : (a + 1) * BLK] = wide.T.astype(BF16)
    scale = 1.0 / (jnp.sqrt(trace) + EPSILON)
    scale2 = scale * scale

    def rows_of(t):
        return slice(t * BLK, (t + 1) * BLK)

    for t in range(3):
        square = dot(gram[rows_of(t)], gram[...])
        poly[rows_of(t)] = (
            (COEFF_B * scale2) * gram[rows_of(t)].astype(F32)
            + (COEFF_C * scale2 * scale2) * square
        ).astype(BF16)
    for t in range(3):
        value = scale2 * (
            COEFF_A * gram[rows_of(t)].astype(F32) + dot(poly[rows_of(t)], gram[...])
        )
        hmat[rows_of(t)] = value
        hmat16[rows_of(t)] = value.astype(BF16)
    for t in range(2):
        value = COEFF_A * xs[rows_of(t)].astype(F32) + dot(xs[rows_of(t)], poly[...])
        x1[rows_of(t)] = (scale * value).astype(BF16)
    for t in range(3):
        value = COEFF_A * hmat[rows_of(t)] + dot(hmat16[rows_of(t)], poly[...])
        gram[rows_of(t)] = value.astype(BF16)
    for t in range(3):
        square = dot(gram[rows_of(t)], gram[...])
        hmat16[rows_of(t)] = (
            COEFF_B * gram[rows_of(t)].astype(F32) + COEFF_C * square
        ).astype(BF16)
    for t in range(2):
        value = COEFF_A * x1[rows_of(t)].astype(F32) + dot(x1[rows_of(t)], hmat16[...])
        update[rows_of(t)] = (math.sqrt(D) * value.astype(BF16).astype(F32)).astype(BF16)

    for copy in swaps + [idx_swap] + pending:
        copy.wait_send()
    for pos in range(4):
        rest = a_send.at[pos, pl.ds(0, (PLANE - 1) * CAP)]
        pltpu.make_async_copy(rest, rest, a_send_sem.at[pos]).wait()

    def idx_done(i, carry):
        to = lax.rem(q + i, PLANE)
        pltpu.make_async_copy(idx_send.at[to], idx_send.at[to], idx_all_send.at[to]).wait()
        return carry

    lax.fori_loop(1, PLANE, idx_done, 0)


def body(activations, out_grad, gate_weights, routes, momentum):
    vmem = pl.BlockSpec(memory_space=pltpu.VMEM)
    dma = pltpu.SemaphoreType.DMA
    scratch = [
        pltpu.VMEM((ROWS, FF), F32),
        pltpu.VMEM((2, 2, TOK, ROWS), BF16),
        pltpu.VMEM((2, PLANE, ROWS, 2 * TOK), BF16),
        pltpu.VMEM((4, PLANE * CAP, FF), BF16),
        pltpu.VMEM((4, 4, 2, 4 * CAP, FF), BF16),
        pltpu.VMEM((PLANE, PAIRS), F32),
        pltpu.VMEM((PLANE, PAIRS), F32),
        pltpu.VMEM((PLANE, 1, PAIRS), F32),
        pltpu.VMEM((PLANE, 1, PAIRS), F32),
        pltpu.VMEM((4, PAIRS, PAIRS), BF16),
        pltpu.VMEM((4, 2, ROWS, PAIRS), BF16),
        pltpu.VMEM((2, 2, HALF, FF), BF16),
        pltpu.VMEM((2, 7, HALF, FF), BF16),
        pltpu.VMEM((ROWS, FF), BF16),
        pltpu.VMEM((2, 3, BLK, BLK), F32),
        pltpu.VMEM((3, BLK, BLK), BF16),
        pltpu.VMEM((3, BLK, BLK), BF16),
        pltpu.VMEM((3, BLK, BLK), BF16),
        pltpu.VMEM((3, BLK, BLK), BF16),
        pltpu.VMEM((2, 3, BLK, BLK), BF16),
        pltpu.VMEM((FF, FF), BF16),
        pltpu.VMEM((FF, FF), BF16),
        pltpu.VMEM((FF, FF), F32),
        pltpu.VMEM((FF, FF), BF16),
        pltpu.VMEM((ROWS, FF), BF16),
        dma((3,)),
        dma((2,)),
        dma((2,)),
        dma((2, 15)),
        dma((2, 15)),
        dma((4,)),
        dma((4,)),
        dma((4,)),
        dma((4,)),
        dma((4,)),
        dma((2,)),
        dma((PLANE,)),
        dma((PLANE,)),
        dma((2, 7)),
        dma((2, 7)),
        dma((3,)),
        dma((3,)),
    ]
    return pl.pallas_call(
        kernel,
        out_shape=(
            jax.ShapeDtypeStruct((ROWS, FF), BF16),
            jax.ShapeDtypeStruct((ROWS, FF), F32),
        ),
        in_specs=[vmem] * 4 + [pl.BlockSpec(memory_space=pl.ANY)],
        out_specs=(vmem, vmem),
        scratch_shapes=scratch,
        compiler_params=pltpu.CompilerParams(
            collective_id=0, has_side_effects=True, vmem_limit_bytes=56 * 2**20
        ),
    )(activations.reshape(PAIRS, FF), out_grad, gate_weights, routes, momentum)


def solution(mesh):
    in_specs = (
        P(("dp", "expert"), None, None),
        P(("dp", "expert"), None),
        P(("dp", "expert"), None),
        P(("dp", "expert"), None),
        P(("expert", "dp"), None),
    )
    out_specs = (P(("expert", "dp"), None), P(("expert", "dp"), None))
    return jax.shard_map(body, mesh=mesh, in_specs=in_specs, out_specs=out_specs, check_vma=False)
```

time: 350 us -> 144 us (0.41)
  waiting for transfers between devices: 178 us -> 0 us
  Pallas kernels: 0 us -> 137 us
  matrix products: 62.3 us -> 0 us
  local copies, waits for them, and re-layouts: 39 us -> 6.1 us
  other arithmetic: 28 us -> 0 us
  starting transfers between devices: 14.9 us -> 0 us
  between operations: 15 us -> 0.65 us
  loops' own time: 11.1 us -> 0 us
    pallas_call x0 -> x1, Pallas kernels: none -> 137 us  [body(): pl.pallas_call(kernel, out_shape=(jax.ShapeDtypeStruct((ROWS, FF), BF16),...]
    reduce_scatter x1 -> x0, waiting for transfers between devices: 86.8 us -> none  [body(): lax.psum_scatter(blocks.reshape(own_rows * lax.axis_size('dp'), hidden_wi...]
    dot_general x20 -> x0, matrix products: 62.3 us -> none  [the longest x16 38.2 us: block_rows(): lax.dot_general(columns, hidden_expert, (((0,), (0,)), ((), ())), preferr...]
    all_to_all x2 -> x0, waiting for transfers between devices: 53.5 us -> none  [the longest x1 47 us: body(): lax.all_to_all(weighted_send, 'expert', split_axis=1, concat_axis=1, tile...]
    ppermute x2 -> x0, waiting for transfers between devices: 37.8 us -> none  [swapped(): return lax.ppermute(block, axis, route)]
    convert_element_type x7 -> x0, other arithmetic: 20.8 us -> none  [the longest x1 7.74 us: pack_slots(): weighted = (scales[..., None] * grad_rows).astype(jnp.bfloat16)]
    gather x4 -> x0, local copies, waits for them, and re-layouts: 16.9 us -> none  [the longest x2 6.88 us: pack_slots(): jnp.take(gate_block.reshape(-1), source)]
    all_to_all x2 -> x0, starting transfers between devices: 13 us -> none  [the longest x1 7.58 us: body(): lax.all_to_all(hidden_send, 'expert', split_axis=1, concat_axis=1, tiled=...]
  transfers between devices with their start and end apart: 5 -> 0, of which waited for: 5 -> 0; matrix products, arithmetic and copies ran while one was open for 4% -> 0% of each run, Pallas kernels for 0% -> 0%
where the time goes in v1:
time: 144 us; the launch traced here: 143 us
  Pallas kernels  137 us (95%)
  local copies, waits for them, and re-layouts  6.1 us (4%)
    pallas_call x1, Pallas kernels, body(): pl.pallas_call(kernel, out_shape=(jax.ShapeDtypeStruct((ROWS, FF), BF16),...  137 us
    unnamed x6, local copies, waits for them, and re-layouts  6.1 us

profile of v1, /device:TPU:1, one launch (start us, length us, event | category | flops | bytes accessed | tf_op | source)
XLA Modules:
  0.0 143.3 jit_solution(12196571210611749498)
XLA Ops:
  0.6 1.4 copy.7.gate
  2.0 1.4 copy.8.routes
  3.4 136.6 %shard_map.68 = (bf16[512,768]{1,0:T(8,128)(2,1)}, f32[512,768]{1,0:T(8,128)}) custom-call(bf16[512,768]{1,0:T(8,128)(2,1)} %bitcast.1, bf16[64,2048]{1,0:T(8,128)(2,1)} %og.1, f32[64,8]{1,0:T(8,128)} %copy.7.gate, s32[64,8]{1,0:T(8,128)} %copy.8.routes, f32[512,768]{1,0:T(8,128)} %mom_hbm.1), custom_call_target="tpu_custom_call" | custom-call | tf_op jit(solution)/shard_map/pallas_call | solution.py:561
  140.0 0.0 copy-start
  140.0 2.2 %copy.11 = bf16[512,768]{1,0:T(8,128)(2,1)} copy(bf16[512,768]{1,0:T(8,128)(2,1)} %get-tuple-element.4) | data formatting | bytes 1572864
  142.2 0.0 copy-done
  142.2 1.1 copy.12
Async XLA Ops:
  140.0 2.2 %copy-start = (f32[512,768]{1,0:T(8,128)S(1)}, f32[512,768]{1,0:T(8,128)}, u32[]{:S(2)}) copy-start(f32[512,768]{1,0:T(8,128)} %get-tuple-element.5) | copy-start | bytes 4718596

commit v2 on v1

v2 whole, which is shorter than its diff:
```python
import math

import jax
import jax.numpy as jnp
from jax import lax
from jax.experimental import pallas as pl
from jax.experimental.pallas import tpu as pltpu
from jax.sharding import PartitionSpec as P

MOMENT = 0.95
COEFF_A = 3.4445
COEFF_B = -4.775
COEFF_C = 2.0315
EPSILON = 1e-07

F32, BF16, I32 = jnp.float32, jnp.bfloat16, jnp.int32
MESH = pl.DeviceIdType.MESH
D, FF, TOK, TOPK, CAP = 2048, 768, 64, 8, 16
PLANE, RING, SIDE = 16, 8, 4
PAIRS = TOK * TOPK
ROWS = 512
SPLIT = 2
CHUNK = ROWS // SPLIT
PIECE = CHUNK // 2
ORDER = (
    "P0", "G00", "G01", "G02", "B0", "B1", "P1", "G10", "G11", "G12", "I0", "M0", "M1", "I1",
    "E0", "E1", "W0", "I2", "F0", "A0", "S00", "B2", "P2", "G20", "G21", "G22", "W1", "F1",
    "A1", "S10", "S20", "B3", "M2", "W2", "A2", "S30", "M3", "E2", "P3", "G30", "G31", "G32",
    "S40", "E3", "F2", "S01", "W3", "A3", "S50", "F3", "S11", "S60", "S21", "S31", "S41", "S51",
    "S61",
)
BLK = 256
SPREAD = (
    ((1, 0), (-1, 0), (0, 1), (0, -1), (1, 1), (-1, -1), (1, -1), (-1, 1))
    + ((2, 0), (0, 2), (2, 1), (1, 2), (2, -1), (-1, 2), (2, 2))
)
PARTS = (((0, 0), (0, 1), (1, 1)), ((0, 2), (1, 2), (2, 2)))


def iota(shape, dim):
    return lax.broadcasted_iota(I32, shape, dim)


def dot(a, b):
    return jnp.dot(a, b, preferred_element_type=F32)


def kernel(
    act_hbm,
    og,
    gate,
    routes,
    mom_hbm,
    xs_out,
    mom_out,
    gram_out,
    act,
    mom,
    ogx,
    og_buf,
    a_send,
    a_buf,
    idx_mine,
    idx_peer,
    idx_send,
    idx_buf,
    sel,
    wt,
    first,
    ring,
    xs,
    gram_send,
    gram_core,
    gram_own,
    gram_sum,
    gram_z,
    gram_tot,
    local_sem,
    ogx_send,
    ogx_recv,
    og_send,
    og_recv,
    a_send_sem,
    a_recv_sem,
    a_own_sem,
    ap_send,
    ap_recv,
    idx_sems,
    idx_all_send,
    idx_all_recv,
    z_send,
    z_recv,
    g_send,
    g_recv,
):
    dp = lax.axis_index("dp")
    q = lax.axis_index("expert")
    z, c = lax.div(dp, 2), lax.rem(dp, 2)
    g0, zo = lax.div(z, 2), lax.rem(z, 2)
    qx, qy = lax.div(q, SIDE), lax.rem(q, SIDE)
    peer = 2 * z + 1 - c
    zr = 2 * lax.rem(z + 1, RING) + c
    zl = 2 * lax.rem(z + RING - 1, RING) + c
    zpair = 2 * (2 * g0 + 1 - zo) + c

    def send(src, dst, s_sem, r_sem, to_dp, to_q):
        copy = pltpu.make_async_remote_copy(
            src_ref=src,
            dst_ref=dst,
            send_sem=s_sem,
            recv_sem=r_sem,
            device_id=(to_dp, to_q),
            device_id_type=MESH,
        )
        copy.start()
        return copy

    pending = []
    mom_copy = pltpu.make_async_copy(mom_hbm, mom, local_sem.at[0])
    mom_copy.start()
    act_copy = pltpu.make_async_copy(act_hbm, act, local_sem.at[6])
    act_copy.start()

    barrier = pltpu.get_barrier_semaphore()

    def greet(i, carry):
        pl.semaphore_signal(
            barrier, inc=1, device_id=(dp, lax.rem(q + i, PLANE)), device_id_type=MESH
        )
        return carry

    lax.fori_loop(1, PLANE, greet, 0)
    for other in (peer, zr, zl):
        pl.semaphore_signal(barrier, inc=1, device_id=(other, q), device_id_type=MESH)
    pl.semaphore_wait(barrier, PLANE + 2)

    swaps, owns = [], []
    for o in range(2):
        zp = zo if o == 0 else 1 - zo
        mine = pl.multiple_of((2 * zp + c) * ROWS, ROWS)
        theirs = pl.multiple_of((2 * zp + 1 - c) * ROWS, ROWS)
        swaps.append(
            send(
                og.at[:, pl.ds(theirs, ROWS)],
                ogx.at[o, c],
                ogx_send.at[o],
                ogx_recv.at[o],
                peer,
                q,
            )
        )
        own = pltpu.make_async_copy(
            og.at[:, pl.ds(mine, ROWS)], ogx.at[o, c], local_sem.at[1 + o]
        )
        own.start()
        owns.append(own)

    spread = (lax.shift_right_logical(iota((TOK, PAIRS), 1), 3) == iota((TOK, PAIRS), 0)).astype(
        F32
    )
    own_k = (iota((TOPK, PAIRS), 1) & 7) == iota((TOPK, PAIRS), 0)

    def as_row(values):
        wide = jnp.dot(
            values, spread, precision=lax.Precision.HIGHEST, preferred_element_type=F32
        )
        return jnp.sum(jnp.where(own_k, wide, 0.0), axis=0, keepdims=True)

    route_row = as_row(routes[...].astype(F32))
    gate_row = as_row(gate[...])
    named = iota((TOK, PAIRS), 0).astype(F32) == route_row
    before = lax.shift_right_logical(iota((PAIRS, PAIRS), 0), 3) < lax.shift_right_logical(
        iota((PAIRS, PAIRS), 1), 3
    )
    counts = dot(named.astype(F32).astype(BF16), before.astype(F32).astype(BF16))
    place = jnp.sum(jnp.where(named, counts, 0.0), axis=0, keepdims=True)
    route_int = route_row.astype(I32)
    place_int = place.astype(I32)
    route_low, route_high = route_int & 3, lax.shift_right_logical(route_int, 2)
    slot = route_low * (PLANE * CAP) + route_high * CAP + place_int

    g_at = (
        lax.rem(g0 + 2, 4),
        lax.rem(g0 + 1 + 2 * zo, 4),
        lax.rem(g0 + 3 - 2 * zo, 4),
        g0,
    )

    u, v = (1 - c) * qx + c * qy, (1 - c) * qy + c * qx

    def at(du, dv):
        uu, vv = lax.rem(u + du + SIDE, SIDE), lax.rem(v + dv + SIDE, SIDE)
        return (1 - c) * (SIDE * uu + vv) + c * (SIDE * vv + uu)

    def pack(pos):
        if pos == 0:
            act_copy.wait()
        hit = (iota((PLANE * CAP, PAIRS), 0) + g_at[pos] * (PLANE * CAP)) == slot
        picked = dot(hit.astype(F32).astype(BF16), act[...])
        scale = jnp.sum(jnp.where(hit, gate_row, 0.0), axis=1, keepdims=True)
        a_send[pos] = (picked * scale).astype(BF16)

    def give(both):
        pos, third = both // 10, both % 10
        for du, dv in SPREAD[5 * third : 5 * third + 5]:
            to = at(du, dv)
            send(
                a_send.at[pos, pl.ds(pl.multiple_of(to * CAP, CAP), CAP)],
                a_buf.at[pos, qx, c, pl.ds(pl.multiple_of(qy * CAP, CAP), CAP)],
                a_send_sem.at[pos],
                a_recv_sem.at[pos],
                dp,
                to,
            )
        if third == 2:
            pltpu.make_async_copy(
                a_send.at[pos, pl.ds(pl.multiple_of(q * CAP, CAP), CAP)],
                a_buf.at[pos, qx, c, pl.ds(pl.multiple_of(qy * CAP, CAP), CAP)],
                a_own_sem.at[pos],
            ).start()

    def forward(pos):
        rest = a_send.at[pos, pl.ds(0, (PLANE - 1) * CAP)]
        pltpu.make_async_copy(rest, rest, a_recv_sem.at[pos]).wait()
        piece = a_send.at[pos, pl.ds(0, CAP)]
        pltpu.make_async_copy(piece, piece, a_own_sem.at[pos]).wait()
        copy = send(
            a_buf.at[pos, :, c], a_buf.at[pos, :, c], ap_send.at[pos], ap_recv.at[pos], peer, q
        )
        pending.append(copy)
        return copy

    def og_send_one(o, source, to, key):
        send(
            og_buf.at[o, source],
            og_buf.at[o, source],
            og_send.at[o],
            og_recv.at[o, key],
            dp,
            to,
        )

    def og_wait(o, source, key):
        pltpu.make_async_remote_copy(
            src_ref=og_buf.at[o, source],
            dst_ref=og_buf.at[o, source],
            send_sem=og_send.at[o],
            recv_sem=og_recv.at[o, key],
            device_id=(dp, q),
            device_id_type=MESH,
        ).wait_recv()

    k_du = (0, -1, 1, 2)

    def og_begin(o):
        if o < 2:
            swaps[o].wait_recv()
            owns[o].wait()
        cols = slice((o // 2) * CHUNK, (o // 2 + 1) * CHUNK)
        og_buf[o, q] = ogx[o % 2, :, :, cols].reshape(2 * TOK, CHUNK).T
        og_send_one(o, q, at(1, 0), 0)
        og_send_one(o, q, at(-1, 0), 1)
        og_send_one(o, q, at(0, 1), 3)
        og_send_one(o, q, at(0, -1), 7)

    def og_second(o, k):
        source = at(k_du[k], 0)
        og_send_one(o, source, at(0, 1), 3 + k)
        og_send_one(o, source, at(0, -1), 7 + k)

    def og_relay(o, k):
        if k < 2:
            og_wait(o, at(k_du[k], -1), 3 + k)
            og_send_one(o, at(k_du[k], -1), at(0, 1), 11 + k)
        else:
            og_wait(o, at(k_du[k], 1), 7 + k)
            og_send_one(o, at(k_du[k], 1), at(0, -1), 11 + k)

    def og_middle(o):
        og_wait(o, at(-1, 0), 0)
        if (o // 2 + o) % 2 == 0:
            og_send_one(o, at(-1, 0), at(1, 0), 2)
        og_second(o, 1)
        og_wait(o, at(1, 0), 1)
        if (o // 2 + o) % 2 == 1:
            og_send_one(o, at(1, 0), at(-1, 0), 2)
        og_second(o, 2)
        og_relay(o, 0)

    def og_end(o):
        og_wait(o, at(2, 0), 2)
        og_second(o, 3)
        for k in (1, 2, 3):
            og_relay(o, k)

    def og_all(o):
        for k in (2, 3):
            og_wait(o, at(k_du[k], -1), 3 + k)
        for k in (0, 1):
            og_wait(o, at(k_du[k], 1), 7 + k)
        for k in range(4):
            og_wait(o, at(k_du[k], 2), 11 + k)

    swapped = []

    def idx_begin():
        key_row = route_low * CAP + place_int
        token = lax.shift_right_logical(iota((TOK, PAIRS), 1), 3) + 1 + TOK * c
        key_hot = (
            jnp.where(iota((TOK, PAIRS), 0) == key_row, token, 0).astype(F32).astype(BF16)
        )
        high_hot = (iota((PLANE, PAIRS), 0) == route_high).astype(F32).astype(BF16)
        tokens = lax.dot_general(
            high_hot, key_hot, (((1,), (1,)), ((), ())), preferred_element_type=F32
        )
        lane = iota((TOK, PAIRS), 1)
        lane_key = lax.shift_right_logical(lane, 7) * CAP + (lane & 15)
        lane_mine = ((lax.shift_right_logical(lane, 6) & 1) == c) & (
            (lax.shift_right_logical(lane, 4) & 3) == qy
        )
        widen = (lane_mine & (lane_key == iota((TOK, PAIRS), 0))).astype(F32).astype(BF16)
        idx_mine[...] = dot(tokens.astype(BF16), widen)
        swapped.append(send(idx_mine, idx_peer, idx_sems.at[0], idx_sems.at[1], peer, q))

    def idx_share():
        swapped[0].wait_recv()
        both = idx_mine[...] + idx_peer[...]
        for i in range(PLANE):
            idx_send[i] = both[i : i + 1]

        def one(i, carry):
            to = lax.rem(q + i, PLANE)
            send(idx_send.at[to], idx_buf.at[q], idx_all_send.at[to], idx_all_recv.at[q], dp, to)
            return carry

        lax.fori_loop(1, PLANE, one, 0)
        idx_buf[q] = idx_send[q]

    def idx_end():
        def one(i, carry):
            source = lax.rem(q + i, PLANE)
            pltpu.make_async_copy(
                idx_buf.at[source], idx_buf.at[source], idx_all_recv.at[source]
            ).wait()
            return carry

        lax.fori_loop(1, PLANE, one, 0)
        for grp in range(4):
            for j in range(4):
                hit = (iota((2 * TOK, PAIRS), 0) + 1).astype(F32) == idx_buf[4 * grp + j]
                sel[grp, j * 128 : (j + 1) * 128] = hit.astype(F32).astype(BF16)

    def pick(o):
        rows = slice((o // 2) * CHUNK, (o // 2 + 1) * CHUNK)
        for grp in range(4):
            left = jnp.concatenate([og_buf[o, 4 * grp + j] for j in range(4)], axis=1)
            out = dot(left, sel[grp]).astype(BF16)
            for g in range(4):
                wt[g, o % 2, rows, grp * 128 : (grp + 1) * 128] = out[:, g * 128 : (g + 1) * 128]

    def partial(g, o, pos, low, n):
        cols = slice(n * BLK, (n + 1) * BLK)
        return dot(wt[g, o, low : low + PIECE], a_buf[pos, :, :, :, cols].reshape(PAIRS, BLK))

    def low_row(h, way, s):
        return s * CHUNK + PIECE * ((h + way) % 2)

    def step(h, s):
        dist = (4, 3, 3, 2, 2, 1, 1)[h]
        o = (0, 1, 1, 0, 0, 1, 1)[h]
        place_right = (0, 1 - zo, 1 - zo, 1 + zo, 1 + zo, 3 - zo, 3 - zo)[h]
        place_left = (0, zo, zo, 2 - zo, 2 - zo, 2 + zo, 2 + zo)[h]
        for way in range(2):
            dest = lax.rem(z + (dist if way == 0 else RING - dist), RING)
            g = lax.div(dest, 2)
            pos = place_right if way == 0 else place_left
            target = first.at[way, h, s] if h < 2 else ring.at[way, h - 2, s]
            if h >= 2:
                z_copies[way, h - 2, s].wait_recv()
            for n in range(3):
                cols = slice(n * BLK, (n + 1) * BLK)
                value = partial(g, o, pos, low_row(h, way, s), n)
                if h >= 2:
                    value = value + ring[way, h - 2, s, :, cols].astype(F32)
                target[:, cols] = value.astype(BF16)
            copy = send(
                target,
                ring.at[way, h, s],
                z_send.at[way, h, s],
                z_recv.at[way, h, s],
                zr if way == 0 else zl,
                q,
            )
            pending.append(copy)
            z_copies[way, h, s] = copy

    z_copies, arrive = {}, {}

    def og_final(o):
        og_all(o)
        pick(o)

    def pass_on(pos):
        arrive[pos] = forward(pos)

    def have(pos):
        arrive[pos].wait_recv()

    index = (idx_begin, idx_share, idx_end)
    work = {
        "P": pack,
        "G": give,
        "B": og_begin,
        "M": og_middle,
        "E": og_end,
        "F": og_final,
        "W": pass_on,
        "A": have,
        "I": lambda i: index[i](),
        "S": lambda both: step(both // 10, both % 10),
    }
    for name in ORDER:
        work[name[0]](int(name[1:]))

    def block_of(half, i, s):
        a, b = ((0, 2 * half), (half, 1 + half), (1 + half, 1 + half))[i]
        rows = slice(s * CHUNK, (s + 1) * CHUNK)
        return lax.dot_general(
            xs[rows, pl.ds(pl.multiple_of(a * BLK, BLK), BLK)],
            xs[rows, pl.ds(pl.multiple_of(b * BLK, BLK), BLK)],
            (((0,), (0,)), ((), ())),
            preferred_element_type=F32,
        )

    mom_copy.wait()
    for s in range(SPLIT):
        for way in range(2):
            z_copies[way, 5, s].wait_recv()
        for way in range(2):
            z_copies[way, 6, s].wait_recv()
        for odd in range(2):
            low = s * CHUNK + odd * PIECE
            rows = slice(low, low + PIECE)
            for n in range(3):
                cols = slice(n * BLK, (n + 1) * BLK)
                gradient = (
                    partial(g0, 0, 3, low, n)
                    + ring[0, 6 - odd, s, :, cols].astype(F32)
                    + ring[1, 5 + odd, s, :, cols].astype(F32)
                )
                momentum = MOMENT * mom[rows, cols] + gradient
                mom[rows, cols] = momentum
                xs[rows, cols] = (gradient + MOMENT * momentum).astype(BF16)
        if s < SPLIT - 1:
            for half in range(2):
                for i in range(3):
                    value = block_of(half, i, s)
                    gram_own[half, i] = value if s == 0 else gram_own[half, i] + value
    to_core, to_z, back = [], [], []
    for i in range(3):
        gram_send[i] = (gram_own[1 - c, i] + block_of(1 - c, i, SPLIT - 1)).astype(BF16)
        to_core.append(
            send(gram_send.at[i], gram_core.at[i], g_send.at[0, i], g_recv.at[0, i], peer, q)
        )
    for i in range(3):
        gram_own[c, i] = gram_own[c, i] + block_of(c, i, SPLIT - 1)
    outs = [
        pltpu.make_async_copy(xs, xs_out, local_sem.at[3]),
        pltpu.make_async_copy(mom, mom_out, local_sem.at[4]),
    ]
    for copy in outs:
        copy.start()
    for i in range(3):
        to_core[i].wait_recv()
        gram_sum[i] = (gram_own[c, i] + gram_core[i].astype(F32)).astype(BF16)
        to_z.append(
            send(gram_sum.at[i], gram_z.at[i], g_send.at[1, i], g_recv.at[1, i], zpair, q)
        )
    for i in range(3):
        to_z[i].wait_recv()
        gram_tot[c, i] = (gram_sum[i].astype(F32) + gram_z[i].astype(F32)).astype(BF16)
        back.append(
            send(
                gram_tot.at[c, i],
                gram_tot.at[c, i],
                g_send.at[2, i],
                g_recv.at[2, i],
                peer,
                q,
            )
        )
    for copy in back:
        copy.wait_recv()
    copy = pltpu.make_async_copy(gram_tot, gram_out, local_sem.at[5])
    copy.start()
    outs.append(copy)

    for copy in swaps + swapped + pending + to_core + to_z + back:
        copy.wait_send()
    for copy in outs:
        copy.wait()
    for pos in range(4):
        rest = a_send.at[pos, pl.ds(0, (PLANE - 1) * CAP)]
        pltpu.make_async_copy(rest, rest, a_send_sem.at[pos]).wait()

    for o in range(2 * SPLIT):
        rest = og_buf.at[o, pl.ds(0, PLANE - 1)]
        pltpu.make_async_copy(rest, rest, og_send.at[o]).wait()

    def idx_done(i, carry):
        to = lax.rem(q + i, PLANE)
        pltpu.make_async_copy(idx_send.at[to], idx_send.at[to], idx_all_send.at[to]).wait()
        return carry

    lax.fori_loop(1, PLANE, idx_done, 0)


def newton(
    xs_hbm, gram_hbm, mom_hbm, update, new_mom, xs, gram_tot, gram, poly, hmat, hmat16, x1, mom, sem
):
    gram_copy = pltpu.make_async_copy(gram_hbm, gram_tot, sem.at[1])
    gram_copy.start()
    xs_copy = pltpu.make_async_copy(xs_hbm, xs, sem.at[2])
    xs_copy.start()
    mom_copy = pltpu.make_async_copy(mom_hbm, mom, sem.at[0])
    mom_copy.start()
    gram_copy.wait()
    trace = jnp.zeros((1, 1), F32)
    eye = iota((BLK, BLK), 0) == iota((BLK, BLK), 1)
    for half in range(2):
        for i, (a, b) in enumerate(PARTS[half]):
            block = gram_tot[half, i]
            gram[a * BLK : (a + 1) * BLK, b * BLK : (b + 1) * BLK] = block
            wide = block.astype(F32)
            if a == b:
                trace = trace + jnp.sum(
                    jnp.sum(jnp.where(eye, wide, 0.0), axis=1, keepdims=True), axis=0, keepdims=True
                )
            else:
                gram[b * BLK : (b + 1) * BLK, a * BLK : (a + 1) * BLK] = wide.T.astype(BF16)
    scale = 1.0 / (jnp.sqrt(trace) + EPSILON)
    scale2 = scale * scale

    def rows_of(t):
        return slice(t * BLK, (t + 1) * BLK)

    for t in range(3):
        square = dot(gram[rows_of(t)], gram[...])
        poly[rows_of(t)] = (
            (COEFF_B * scale2) * gram[rows_of(t)].astype(F32)
            + (COEFF_C * scale2 * scale2) * square
        ).astype(BF16)
    for t in range(3):
        value = scale2 * (
            COEFF_A * gram[rows_of(t)].astype(F32) + dot(poly[rows_of(t)], gram[...])
        )
        hmat[rows_of(t)] = value
        hmat16[rows_of(t)] = value.astype(BF16)
    mom_copy.wait()
    mom_back = pltpu.make_async_copy(mom, new_mom, sem.at[0])
    mom_back.start()
    xs_copy.wait()
    for t in range(2):
        value = COEFF_A * xs[rows_of(t)].astype(F32) + dot(xs[rows_of(t)], poly[...])
        x1[rows_of(t)] = (scale * value).astype(BF16)
    for t in range(3):
        value = COEFF_A * hmat[rows_of(t)] + dot(hmat16[rows_of(t)], poly[...])
        gram[rows_of(t)] = value.astype(BF16)
    for t in range(3):
        square = dot(gram[rows_of(t)], gram[...])
        hmat16[rows_of(t)] = (
            COEFF_B * gram[rows_of(t)].astype(F32) + COEFF_C * square
        ).astype(BF16)
    for t in range(2):
        value = COEFF_A * x1[rows_of(t)].astype(F32) + dot(x1[rows_of(t)], hmat16[...])
        update[rows_of(t)] = (math.sqrt(D) * value.astype(BF16).astype(F32)).astype(BF16)

    mom_back.wait()


def body(activations, out_grad, gate_weights, routes, momentum):
    vmem = pl.BlockSpec(memory_space=pltpu.VMEM)
    dma = pltpu.SemaphoreType.DMA
    scratch = [
        pltpu.VMEM((PAIRS, FF), BF16),
        pltpu.VMEM((ROWS, FF), F32),
        pltpu.VMEM((2, 2, TOK, ROWS), BF16),
        pltpu.VMEM((2 * SPLIT, PLANE, CHUNK, 2 * TOK), BF16),
        pltpu.VMEM((4, PLANE * CAP, FF), BF16),
        pltpu.VMEM((4, 4, 2, 4 * CAP, FF), BF16),
        pltpu.VMEM((PLANE, PAIRS), F32),
        pltpu.VMEM((PLANE, PAIRS), F32),
        pltpu.VMEM((PLANE, 1, PAIRS), F32),
        pltpu.VMEM((PLANE, 1, PAIRS), F32),
        pltpu.VMEM((4, PAIRS, PAIRS), BF16),
        pltpu.VMEM((4, 2, ROWS, PAIRS), BF16),
        pltpu.VMEM((2, 2, SPLIT, PIECE, FF), BF16),
        pltpu.VMEM((2, 7, SPLIT, PIECE, FF), BF16),
        pltpu.VMEM((ROWS, FF), BF16),
        pltpu.VMEM((3, BLK, BLK), BF16),
        pltpu.VMEM((3, BLK, BLK), BF16),
        pltpu.VMEM((2, 3, BLK, BLK), F32),
        pltpu.VMEM((3, BLK, BLK), BF16),
        pltpu.VMEM((3, BLK, BLK), BF16),
        pltpu.VMEM((2, 3, BLK, BLK), BF16),
        dma((7,)),
        dma((2,)),
        dma((2,)),
        dma((2 * SPLIT,)),
        dma((2 * SPLIT, 15)),
        dma((4,)),
        dma((4,)),
        dma((4,)),
        dma((4,)),
        dma((4,)),
        dma((2,)),
        dma((PLANE,)),
        dma((PLANE,)),
        dma((2, 7, SPLIT)),
        dma((2, 7, SPLIT)),
        dma((3, 3)),
        dma((3, 3)),
    ]
    hbm = pl.BlockSpec(memory_space=pltpu.HBM)
    xs, moved, gram_tot = pl.pallas_call(
        kernel,
        out_shape=(
            jax.ShapeDtypeStruct((ROWS, FF), BF16),
            jax.ShapeDtypeStruct((ROWS, FF), F32),
            jax.ShapeDtypeStruct((2, 3, BLK, BLK), BF16),
        ),
        in_specs=[hbm, hbm, vmem, vmem, hbm],
        out_specs=(hbm, hbm, hbm),
        scratch_shapes=scratch,
        compiler_params=pltpu.CompilerParams(
            collective_id=0, has_side_effects=True, vmem_limit_bytes=60 * 2**20
        ),
    )(activations.reshape(PAIRS, FF), out_grad, gate_weights.T, routes.T, momentum)
    return pl.pallas_call(
        newton,
        out_shape=(
            jax.ShapeDtypeStruct((ROWS, FF), BF16),
            jax.ShapeDtypeStruct((ROWS, FF), F32),
        ),
        in_specs=[hbm, hbm, hbm],
        out_specs=(vmem, hbm),
        scratch_shapes=[
            pltpu.VMEM((ROWS, FF), BF16),
            pltpu.VMEM((2, 3, BLK, BLK), BF16),
            pltpu.VMEM((FF, FF), BF16),
            pltpu.VMEM((FF, FF), BF16),
            pltpu.VMEM((FF, FF), F32),
            pltpu.VMEM((FF, FF), BF16),
            pltpu.VMEM((ROWS, FF), BF16),
            pltpu.VMEM((ROWS, FF), F32),
            dma((3,)),
        ],
        compiler_params=pltpu.CompilerParams(vmem_limit_bytes=60 * 2**20),
    )(xs, gram_tot, moved)


def solution(mesh):
    in_specs = (
        P(("dp", "expert"), None, None),
        P(("dp", "expert"), None),
        P(("dp", "expert"), None),
        P(("dp", "expert"), None),
        P(("expert", "dp"), None),
    )
    out_specs = (P(("expert", "dp"), None), P(("expert", "dp"), None))
    return jax.shard_map(body, mesh=mesh, in_specs=in_specs, out_specs=out_specs, check_vma=False)
```

time: 144 us -> 125 us (0.87)
  Pallas kernels: 137 us -> 123 us
  local copies, waits for them, and re-layouts: 6.1 us -> 0 us
    pallas_call x1, Pallas kernels: 137 us -> 116 us  [body(): pl.pallas_call(kernel, out_shape=(jax.ShapeDtypeStruct((ROWS, FF), BF16),...]
    pallas_call x0 -> x1, Pallas kernels: none -> 7.44 us  [body(): pl.pallas_call(newton, out_shape=(jax.ShapeDtypeStruct((ROWS, FF), BF16),...]
    unnamed x6 -> x0, local copies, waits for them, and re-layouts: 6.1 us -> none
where the time goes in v2:
time: 125 us; the launch traced here: 124 us
  Pallas kernels  123 us (98%)
    pallas_call x1, Pallas kernels, body(): pl.pallas_call(kernel, out_shape=(jax.ShapeDtypeStruct((ROWS, FF), BF16),...  116 us
    pallas_call x1, Pallas kernels, body(): pl.pallas_call(newton, out_shape=(jax.ShapeDtypeStruct((ROWS, FF), BF16),...  7.44 us

profile of v2, /device:TPU:1, one launch (start us, length us, event | category | flops | bytes accessed | tf_op | source)
XLA Modules:
  0.0 124.0 jit_solution(13587754897767601754)
XLA Ops:
  0.6 115.7 %shard_map.68 = (bf16[512,768]{1,0:T(8,128)(2,1)}, f32[512,768]{1,0:T(8,128)}, bf16[2,3,256,256]{3,2,1,0:T(8,128)(2,1)}) custom-call(bf16[512,768]{1,0:T(8,128)(2,1)} %bitcast.3, bf16[64,2048]{1,0:T(8,128)(2,1)} %og.1, f32[8,64]{1,0:T(8,128)} %bitcast.4, s32[8,64]{1,0:T(8,128)} %bitcast.5, f32[512,768]{1,0:T(8,128)} %mom_hbm.1), custom_call_target="tpu_custom_call" | custom-call | tf_op jit(solution)/shard_map/pallas_call | solution.py:625
  116.3 7.4 %shard_map.69 = (bf16[512,768]{1,0:T(8,128)(2,1)}, f32[512,768]{1,0:T(8,128)}) custom-call(bf16[512,768]{1,0:T(8,128)(2,1)} %get-tuple-element.5.xs_hbm, bf16[2,3,256,256]{3,2,1,0:T(8,128)(2,1)} %get-tuple-element.6.gram_hbm, f32[512,768]{1,0:T(8,128)} %get-tuple-element.7.mom_hbm), custom_call_target="tpu_custom_call" | custom-call | tf_op jit(solution)/shard_map/pallas_call | solution.py:639

commit v3 on v2

--- a/solution.py
+++ b/solution.py
@@ -23,10 +23,10 @@
 CHUNK = ROWS // SPLIT
 PIECE = CHUNK // 2
 ORDER = (
-    "P0", "G00", "G01", "G02", "B0", "B1", "P1", "G10", "G11", "G12", "I0", "M0", "M1", "I1",
-    "E0", "E1", "W0", "I2", "F0", "A0", "S00", "B2", "P2", "G20", "G21", "G22", "W1", "F1",
-    "A1", "S10", "S20", "B3", "M2", "W2", "A2", "S30", "M3", "E2", "P3", "G30", "G31", "G32",
-    "S40", "E3", "F2", "S01", "W3", "A3", "S50", "F3", "S11", "S60", "S21", "S31", "S41", "S51",
+    "B0", "P0", "G00", "G01", "G02", "B1", "I0", "M0", "I1", "M1", "E0", "W0", "P1", "G10",
+    "G11", "G12", "I2", "E1", "P2", "G20", "G21", "G22", "F0", "A0", "S00", "W1", "P3", "G30",
+    "G31", "G32", "B2", "F1", "A1", "S10", "S20", "B3", "M2", "W2", "A2", "S30", "M3", "E2",
+    "W3", "S40", "E3", "A3", "F2", "S50", "S01", "S60", "F3", "S11", "S21", "S31", "S41", "S51",
     "S61",
 )
 BLK = 256

time: 125 us -> 124 us (level)
  no operation moved by 1% of the time
where the time goes in v3:
time: 124 us
  Pallas kernels  123 us (99%)
    pallas_call x1, Pallas kernels, body(): pl.pallas_call(kernel, out_shape=(jax.ShapeDtypeStruct((ROWS, FF), BF16),...  116 us
    pallas_call x1, Pallas kernels, body(): pl.pallas_call(newton, out_shape=(jax.ShapeDtypeStruct((ROWS, FF), BF16),...  7.44 us

profile of v3, /device:TPU:1, one launch (start us, length us, event | category | flops | bytes accessed | tf_op | source)
XLA Modules:
  0.0 123.8 jit_solution(4820373006306333512)
XLA Ops:
  0.6 115.6 %shard_map.68 = (bf16[512,768]{1,0:T(8,128)(2,1)}, f32[512,768]{1,0:T(8,128)}, bf16[2,3,256,256]{3,2,1,0:T(8,128)(2,1)}) custom-call(bf16[512,768]{1,0:T(8,128)(2,1)} %bitcast.3, bf16[64,2048]{1,0:T(8,128)(2,1)} %og.1, f32[8,64]{1,0:T(8,128)} %bitcast.4, s32[8,64]{1,0:T(8,128)} %bitcast.5, f32[512,768]{1,0:T(8,128)} %mom_hbm.1), custom_call_target="tpu_custom_call" | custom-call | tf_op jit(solution)/shard_map/pallas_call | solution.py:625
  116.2 7.4 %shard_map.69 = (bf16[512,768]{1,0:T(8,128)(2,1)}, f32[512,768]{1,0:T(8,128)}) custom-call(bf16[512,768]{1,0:T(8,128)(2,1)} %get-tuple-element.5.xs_hbm, bf16[2,3,256,256]{3,2,1,0:T(8,128)(2,1)} %get-tuple-element.6.gram_hbm, f32[512,768]{1,0:T(8,128)} %get-tuple-element.7.mom_hbm), custom_call_target="tpu_custom_call" | custom-call | tf_op jit(solution)/shard_map/pallas_call | solution.py:639
